TPU v7x, 512 devices: a whole 4x8x8 slice. The times are simulated.
512 devices in a mesh: dp: 32 (over y_lo, z, core), row: 4 (over y_hi), col: 4 (over x).
Axes of the slice: x: 4, y: 8 (y_hi: 4, y_lo: 2; y = y_hi * 2 + y_lo), z: 8, core: 2. Of those that a mesh axis runs over, the one named last changes fastest.
Arguments:
- heads_out: bfloat16 [8192, 6144], P(('dp', 'col'), 'row'), may hold values from -6 to 6
- residual: bfloat16 [8192, 6144], P('dp', 'col'), may hold values from -6 to 6
- master: float32 [6144, 6144], P(('row', 'dp'), 'col'), may hold values from -6 to 6
- moment_one: float32 [6144, 6144], P(('row', 'dp'), 'col'), may hold values from -4 to 4
- moment_two: float32 [6144, 6144], P(('row', 'dp'), 'col'), may hold values from 0.05 to 2
- out_grad: bfloat16 [8192, 6144], P('dp', 'col'), may hold values from -6 to 6
Outputs:
- stream_out: bfloat16 [8192, 6144], P('dp', 'col')
- heads_grad: bfloat16 [8192, 6144], P(('dp', 'col'), 'row')
- weight_grad: float32 [6144, 6144], P(('row', 'dp'), 'col')
- new_master: float32 [6144, 6144], P(('row', 'dp'), 'col')
- new_moment_one: float32 [6144, 6144], P(('row', 'dp'), 'col')
- new_moment_two: float32 [6144, 6144], P(('row', 'dp'), 'col')
All inputs are finite; a program needn't handle non-finite values.
Results may differ from a plain program's by a relative error of at most 0.009.
Values may be sent and summed in bfloat16 or wider, within the bound.
A program may use at most 64 MiB of HBM per device.

v0:
```python
import math
import jax
import jax.numpy as jnp
from jax import lax
from jax.sharding import PartitionSpec as P

HEADS = 48
HEAD_DIM = 128
beta_one = 0.9
beta_two = 0.95
learn_rate = 0.1
weight_decay = 0.1
epsilon = 1e-08


def filled_up(lines, count):
    spare = -len(lines) % count
    return jnp.pad(lines, [(0, spare)] + [(0, 0)] * (lines.ndim - 1))


def sum_by_parts(shard, axis):
    lines = shard.reshape(-1, *shard.shape[1:][-1:])
    padded = filled_up(lines, lax.axis_size(axis))
    own = lax.psum_scatter(padded, axis, scatter_dimension=0, tiled=True)
    whole = lax.all_gather(own, axis, axis=0, tiled=True)
    return whole[: len(lines)].reshape(shard.shape)


def in_blocks(shard, dim, count):
    before, after = (shard.shape[:dim], shard.shape[dim + 1 :])
    return jnp.moveaxis(shard.reshape(*before, count, -1, *after), dim, 0)


def sent_and_summed(shard, axis, dim):
    count = lax.axis_size(axis)
    tiles = lax.all_to_all(in_blocks(shard, dim, count), axis, 0, 0, tiled=True)
    return jnp.sum(tiles.astype(jnp.float32), axis=0)


def owner_grads(gathered, out_grad, fan_scale):
    tile_grad = (
        lax.dot_general(
            gathered, out_grad, (((0,), (0,)), ((), ())), preferred_element_type=jnp.float32
        )
        * fan_scale
    )
    owners = lax.axis_size("dp")
    stacked = tile_grad.astype(jnp.bfloat16).reshape(
        owners, tile_grad.shape[0] // owners, tile_grad.shape[1]
    )
    received = lax.all_to_all(stacked, "dp", split_axis=0, concat_axis=0, tiled=True)
    return jnp.sum(received.astype(jnp.float32), axis=0)


def shards(heads_out, residual, master, moment_one, moment_two, out_grad):
    fan_scale = 1.0 / math.sqrt(HEADS * HEAD_DIM)
    local_weight = master.astype(jnp.bfloat16)
    gathered = lax.all_gather(heads_out, "col", axis=0, tiled=True)
    weight_grad = None
    weight_tile = lax.all_gather(local_weight, "dp", axis=0, tiled=True)
    partial_sum = jnp.dot(gathered, weight_tile, preferred_element_type=jnp.float32) * fan_scale
    head_terms = (
        lax.dot_general(
            out_grad, weight_tile, (((1,), (1,)), ((), ())), preferred_element_type=jnp.float32
        )
        * fan_scale
    )
    mixed_sum = sum_by_parts(partial_sum.astype(jnp.bfloat16), "row").astype(jnp.float32)
    stream_out = (residual.astype(jnp.float32) + mixed_sum).astype(jnp.bfloat16)
    heads_grad = sent_and_summed(head_terms.astype(jnp.bfloat16), "col", 0).astype(jnp.bfloat16)
    weight_grad = owner_grads(gathered, out_grad, fan_scale)
    new_moment_one = beta_one * moment_one + (1.0 - beta_one) * weight_grad
    new_moment_two = beta_two * moment_two + (1.0 - beta_two) * weight_grad * weight_grad
    bias_one = 1.0 - beta_one**10
    bias_two = 1.0 - beta_two**10
    direction = new_moment_one / bias_one / (jnp.sqrt(new_moment_two / bias_two) + epsilon)
    new_master = master - learn_rate * (direction + weight_decay * master)
    return (stream_out, heads_grad, weight_grad, new_master, new_moment_one, new_moment_two)


def solution(mesh):
    return jax.shard_map(
        shards,
        mesh=mesh,
        in_specs=(
            P(("dp", "col"), "row"),
            P("dp", "col"),
            P(("row", "dp"), "col"),
            P(("row", "dp"), "col"),
            P(("row", "dp"), "col"),
            P("dp", "col"),
        ),
        out_specs=(
            P("dp", "col"),
            P(("dp", "col"), "row"),
            P(("row", "dp"), "col"),
            P(("row", "dp"), "col"),
            P(("row", "dp"), "col"),
            P(("row", "dp"), "col"),
        ),
        check_vma=False,
    )
```

profile of v0, /device:TPU:4, one launch (start us, length us, event | category | flops | bytes accessed | tf_op | source)
XLA Modules:
  0.0 276.4 jit_solution(10970078683171486864)
XLA Ops:
  7.2 0.0 copy-start
  7.2 0.0 all-gather.2.cloned.1.call-start
  7.2 17.5 %all_gather.9 = bf16[256,1536]{1,0:T(8,128)(2,1)S(1)} all-gather(bf16[64,1536]{1,0:T(8,128)(2,1)} %param.6), channel_id=1, replica_groups=mesh['dp'=32,'row'=4,'col'=4] {'col'}, dimensions={0}, use_global_device_ids=true | all-gather | bytes 983040 | tf_op jit(solution)/shard_map/all_gather | solution.py:58
  24.7 0.0 copy-done
  24.7 1.4 fusion
  26.1 113.2 %all_to_all.10 = bf16[32,48,1536]{2,1,0:T(8,128)(2,1)S(1)} all-to-all(bf16[32,48,1536]{2,1,0:T(8,128)(2,1)S(1)} %bitcast.8), channel_id=1, replica_groups=mesh['dp'=32,'row'=4,'col'=4] {'dp'}, dimensions={0} | all-to-all | bytes 9437184 | tf_op jit(solution)/shard_map/all_to_all | solution.py:51
  139.3 0.0 copy-start.3
  139.3 0.0 copy-start.4
  139.3 0.0 copy-start.5
  139.3 0.7 convert_reduce_fusion
  140.0 0.3 copy-done.3
  140.3 0.1 copy-done.4
  140.3 0.1 copy-done.5
  140.4 0.0 copy-start.1
  140.4 1.1 multiply_subtract_fusion
  141.6 0.0 all-gather.2.cloned.1.call-update
  141.6 0.0 reduce-scatter.2.cloned.1.call-start
  141.7 69.5 %all-gather.2.cloned.1.call-done = bf16[1536,1536]{1,0:T(8,128)(2,1)} async-done(((bf16[48,1536]{1,0:T(8,128)(2,1)}), bf16[1536,1536]{1,0:T(8,128)(2,1)}) %all-gather.2.cloned.1.call-update) | async-done | bytes 4718608 | tf_op jit(solution)/shard_map/all_gather | solution.py:60
  211.1 4.6 %fusion.1 = bf16[256,1536]{1,0:T(8,128)(2,1)} fusion(bf16[256,1536]{1,0:T(8,128)(2,1)S(1)} %all_gather.9, bf16[1536,1536]{1,0:T(8,128)(2,1)} %all-gather.2.cloned.1.call-done), kind=kOutput, calls=%fused_computation.5 | convolution fusion | flops 1208745984 | bytes 6291456 | tf_op jit(solution)/shard_map/dot_general | solution.py:61
  215.7 0.0 copy-done.1
  215.7 0.0 reduce-scatter.2.cloned.1.call-update
  215.8 0.0 copy-start.2
  215.8 3.8 %fusion.2 = bf16[256,1536]{1,0:T(8,128)(2,1)S(1)} fusion(bf16[256,1536]{1,0:T(8,128)(2,1)S(1)} %copy-done, bf16[1536,1536]{1,0:T(8,128)(2,1)} %all-gather.2.cloned.1.call-done), kind=kOutput, calls=%fused_computation.6 | convolution fusion | flops 1208745984 | bytes 6291456 | tf_op jit(solution)/shard_map/dot_general | solution.py:63
  219.6 14.6 %all_to_all.11 = bf16[4,64,1536]{2,1,0:T(8,128)(2,1)S(1)} all-to-all(bf16[4,64,1536]{2,1,0:T(8,128)(2,1)S(1)} %bitcast.9), channel_id=1, replica_groups=mesh['dp'=32,'row'=4,'col'=4] {'col'}, dimensions={0} | all-to-all | bytes 1572864 | tf_op jit(solution)/shard_map/all_to_all | solution.py:36
  234.2 0.8 reduce_sum.21
  235.0 13.4 %reduce-scatter.2.cloned.1.call-done = bf16[64,1536]{1,0:T(8,128)(2,1)} async-done(((bf16[256,1536]{1,0:T(8,128)(2,1)}), bf16[64,1536]{1,0:T(8,128)(2,1)}) %reduce-scatter.2.cloned.1.call-update) | async-done | bytes 196624 | tf_op jit(solution)/shard_map/reduce_scatter | solution.py:24
  248.4 20.1 %all_gather.11 = bf16[256,1536]{1,0:T(8,128)(2,1)S(1)} all-gather(bf16[64,1536]{1,0:T(8,128)(2,1)} %reduce-scatter.2.cloned.1.call-done), channel_id=1, replica_groups=mesh['dp'=32,'row'=4,'col'=4] {'row'}, dimensions={0}, use_global_device_ids=true | all-gather | bytes 983040 | tf_op jit(solution)/shard_map/all_gather | solution.py:25
  268.5 0.0 copy-done.2
  268.5 1.1 add_convert_fusion
Async XLA Ops:
  7.2 17.5 %copy-start = (bf16[256,1536]{1,0:T(8,128)(2,1)S(1)}, bf16[256,1536]{1,0:T(8,128)(2,1)}, u32[]{:S(2)}) copy-start(bf16[256,1536]{1,0:T(8,128)(2,1)} %param.11) | copy-start | bytes 2359300
  7.2 203.9 %all-gather.2.cloned.1.call-start = ((), (), s32[]{:S(2)}) async-start(), calls=%async_computation.3 | async-start | bytes 4866048 | tf_op jit(solution)/shard_map/all_gather | solution.py:60
  139.3 1.0 copy-start.3
  139.3 1.0 copy-start.4
  139.3 1.1 copy-start.5
  140.4 75.3 %copy-start.1 = (f32[48,1536]{1,0:T(8,128)}, f32[48,1536]{1,0:T(8,128)S(1)}, u32[]{:S(2)}) copy-start(f32[48,1536]{1,0:T(8,128)S(1)} %convert_reduce_fusion) | copy-start | bytes 884740
  141.6 106.7 %reduce-scatter.2.cloned.1.call-start = ((), (), s32[]{:S(2)}) async-start(), calls=%async_computation.4 | async-start | bytes 983040 | tf_op jit(solution)/shard_map/reduce_scatter | solution.py:24
  215.8 52.8 %copy-start.2 = (bf16[256,1536]{1,0:T(8,128)(2,1)S(1)}, bf16[256,1536]{1,0:T(8,128)(2,1)}, u32[]{:S(2)}) copy-start(bf16[256,1536]{1,0:T(8,128)(2,1)} %param.7) | copy-start | bytes 2359300
Sparse Core Ops, SparseCore 0:
  141.7 69.3 all-gather.1
  215.9 32.4 reduce-scatter.1
where the time goes:
time: 277 us; the launch traced here: 276 us
  blocking collectives  165 us (60%)
  waiting for transfers between devices  82.9 us (30%)
  between operations  14.1 us (5%)
  matrix products  9.84 us (4%)
  other arithmetic  3.7 us (1%)
    all_to_all x1, blocking collectives, owner_grads(): lax.all_to_all(stacked, 'dp', split_axis=0, concat_axis=0, tiled=True)  113 us
    all_gather x1, waiting for transfers between devices, shards(): weight_tile = lax.all_gather(local_weight, 'dp', axis=0, tiled=True)  69.5 us
    all_gather x1, blocking collectives, sum_by_parts(): whole = lax.all_gather(own, axis, axis=0, tiled=True)  20.1 us
    all_gather x1, blocking collectives, shards(): gathered = lax.all_gather(heads_out, 'col', axis=0, tiled=True)  17.5 us
    all_to_all x1, blocking collectives, sent_and_summed(): tiles = lax.all_to_all(in_blocks(shard, dim, count), axis, 0, 0, tiled=True)  14.6 us
    reduce_scatter x1, waiting for transfers between devices, sum_by_parts(): own = lax.psum_scatter(padded, axis, scatter_dimension=0, tiled=True)  13.4 us
  transfers between devices with their start and end apart: 2, of which 2 were waited for; matrix products, arithmetic and copies ran while one was open for 2% of the time, Pallas kernels for 0%

commit v1 on v0

--- a/solution.py
+++ b/solution.py
@@ -57,7 +57,10 @@
     local_weight = master.astype(jnp.bfloat16)
     gathered = lax.all_gather(heads_out, "col", axis=0, tiled=True)
     weight_grad = None
-    weight_tile = lax.all_gather(local_weight, "dp", axis=0, tiled=True)
+    size = lax.axis_size("dp")
+    blocks = jnp.stack([local_weight for _ in range(size)])
+    blocks = lax.all_to_all(blocks, "dp", split_axis=0, concat_axis=0)
+    weight_tile = jnp.concatenate(blocks, axis=0)
     partial_sum = jnp.dot(gathered, weight_tile, preferred_element_type=jnp.float32) * fan_scale
     head_terms = (
         lax.dot_general(

time: 277 us -> 319 us (1.15)
  blocking collectives: 165 us -> 279 us
  waiting for transfers between devices: 82.9 us -> 11.5 us
    all_to_all x0 -> x1, blocking collectives: none -> 111 us  [shards(): blocks = lax.all_to_all(blocks, 'dp', split_axis=0, concat_axis=0)]
    all_gather x1 -> x0, waiting for transfers between devices: 69.5 us -> none  [shards(): weight_tile = lax.all_gather(local_weight, 'dp', axis=0, tiled=True)]
  transfers between devices with their start and end apart: 2 -> 1, of which waited for: 2 -> 1; matrix products, arithmetic and copies ran while one was open for 2% -> 1% of each run, Pallas kernels for 0% -> 0%
where the time goes in v1:
time: 319 us; the launch traced here: 318 us
  blocking collectives  279 us (87%)
  between operations  14.1 us (4%)
  waiting for transfers between devices  11.5 us (4%)
  matrix products  7.52 us (2%)
  other arithmetic  3.61 us (1%)
    all_to_all x1, blocking collectives, owner_grads(): lax.all_to_all(stacked, 'dp', split_axis=0, concat_axis=0, tiled=True)  113 us
    all_to_all x1, blocking collectives, shards(): blocks = lax.all_to_all(blocks, 'dp', split_axis=0, concat_axis=0)  111 us
    all_gather x1, blocking collectives, sum_by_parts(): whole = lax.all_gather(own, axis, axis=0, tiled=True)  20.6 us
    all_gather x1, blocking collectives, shards(): gathered = lax.all_gather(heads_out, 'col', axis=0, tiled=True)  17.5 us
    all_to_all x1, blocking collectives, sent_and_summed(): tiles = lax.all_to_all(in_blocks(shard, dim, count), axis, 0, 0, tiled=True)  16 us
    reduce_scatter x1, waiting for transfers between devices, sum_by_parts(): own = lax.psum_scatter(padded, axis, scatter_dimension=0, tiled=True)  11.5 us
  transfers between devices with their start and end apart: 1, of which 1 were waited for; matrix products, arithmetic and copies ran while one was open for 1% of the time, Pallas kernels for 0%

profile of v1, /device:TPU:4, one launch (start us, length us, event | category | flops | bytes accessed | tf_op | source)
XLA Modules:
  0.0 318.4 jit_solution(16528245350887138770)
XLA Ops:
  7.2 0.0 copy-start
  7.2 0.0 reduce-scatter.2.cloned.1.call-start
  7.2 17.5 %all_gather.6 = bf16[256,1536]{1,0:T(8,128)(2,1)S(1)} all-gather(bf16[64,1536]{1,0:T(8,128)(2,1)} %param.6), channel_id=1, replica_groups=mesh['dp'=32,'row'=4,'col'=4] {'col'}, dimensions={0}, use_global_device_ids=true | all-gather | bytes 983040 | tf_op jit(solution)/shard_map/all_gather | solution.py:58
  24.7 0.0 copy-done
  24.7 1.4 fusion
  26.1 113.2 %all_to_all.15 = bf16[32,48,1536]{2,1,0:T(8,128)(2,1)S(1)} all-to-all(bf16[32,48,1536]{2,1,0:T(8,128)(2,1)S(1)} %bitcast.11), channel_id=1, replica_groups=mesh['dp'=32,'row'=4,'col'=4] {'dp'}, dimensions={0} | all-to-all | bytes 9437184 | tf_op jit(solution)/shard_map/all_to_all | solution.py:51
  139.3 0.0 copy-start.4
  139.3 0.0 copy-start.5
  139.3 0.0 copy-start.6
  139.3 0.7 convert_reduce_fusion
  140.0 0.3 copy-done.4
  140.3 0.1 copy-done.5
  140.4 0.1 copy-done.6
  140.4 0.0 copy-start.2
  140.5 1.1 multiply_subtract_fusion
  141.5 0.5 stack.2
  142.0 111.3 %all_to_all.16 = bf16[32,48,1536]{2,1,0:T(8,128)(2,1)S(1)} all-to-all(bf16[32,48,1536]{2,1,0:T(8,128)(2,1)S(1)} %stack.2), channel_id=1, replica_groups=mesh['dp'=32,'row'=4,'col'=4] {'dp'}, dimensions={0} | all-to-all | bytes 9437184 | tf_op jit(solution)/shard_map/all_to_all | solution.py:62
  253.4 0.0 copy-done.2
  253.4 0.0 copy-start.1
  253.4 2.1 copy-done.1
  255.5 2.3 fusion.1
  257.8 0.0 reduce-scatter.2.cloned.1.call-update
  257.8 0.0 copy-start.3
  257.8 3.8 %fusion.2 = bf16[256,1536]{1,0:T(8,128)(2,1)S(1)} fusion(bf16[256,1536]{1,0:T(8,128)(2,1)S(1)} %copy-done, bf16[1536,1536]{1,0:T(8,128)(2,1)} %bitcast.10), kind=kOutput, calls=%fused_computation.6 | convolution fusion | flops 1208745984 | bytes 6291456 | tf_op jit(solution)/shard_map/dot_general | solution.py:66
  261.6 16.0 %all_to_all.17 = bf16[4,64,1536]{2,1,0:T(8,128)(2,1)S(1)} all-to-all(bf16[4,64,1536]{2,1,0:T(8,128)(2,1)S(1)} %bitcast.12), channel_id=1, replica_groups=mesh['dp'=32,'row'=4,'col'=4] {'col'}, dimensions={0} | all-to-all | bytes 1572864 | tf_op jit(solution)/shard_map/all_to_all | solution.py:36
  277.6 0.8 reduce_sum.21
  278.4 11.5 %reduce-scatter.2.cloned.1.call-done = bf16[64,1536]{1,0:T(8,128)(2,1)} async-done(((bf16[256,1536]{1,0:T(8,128)(2,1)}), bf16[64,1536]{1,0:T(8,128)(2,1)}) %reduce-scatter.2.cloned.1.call-update) | async-done | bytes 196624 | tf_op jit(solution)/shard_map/reduce_scatter | solution.py:24
  289.9 20.6 %all_gather.7 = bf16[256,1536]{1,0:T(8,128)(2,1)S(1)} all-gather(bf16[64,1536]{1,0:T(8,128)(2,1)} %reduce-scatter.2.cloned.1.call-done), channel_id=1, replica_groups=mesh['dp'=32,'row'=4,'col'=4] {'row'}, dimensions={0}, use_global_device_ids=true | all-gather | bytes 983040 | tf_op jit(solution)/shard_map/all_gather | solution.py:25
  310.5 0.0 copy-done.3
  310.5 1.1 add_convert_fusion
Async XLA Ops:
  7.2 17.5 %copy-start = (bf16[256,1536]{1,0:T(8,128)(2,1)S(1)}, bf16[256,1536]{1,0:T(8,128)(2,1)}, u32[]{:S(2)}) copy-start(bf16[256,1536]{1,0:T(8,128)(2,1)} %param.11) | copy-start | bytes 2359300
  7.2 282.7 %reduce-scatter.2.cloned.1.call-start = ((), (), s32[]{:S(2)}) async-start(), calls=%async_computation.4 | async-start | bytes 983040 | tf_op jit(solution)/shard_map/reduce_scatter | solution.py:24
  139.3 1.0 copy-start.4
  139.3 1.0 copy-start.5
  139.3 1.1 copy-start.6
  140.4 112.9 %copy-start.2 = (f32[48,1536]{1,0:T(8,128)}, f32[48,1536]{1,0:T(8,128)S(1)}, u32[]{:S(2)}) copy-start(f32[48,1536]{1,0:T(8,128)S(1)} %convert_reduce_fusion) | copy-start | bytes 884740
  253.4 2.1 copy-start.1
  257.8 52.7 %copy-start.3 = (bf16[256,1536]{1,0:T(8,128)(2,1)S(1)}, bf16[256,1536]{1,0:T(8,128)(2,1)}, u32[]{:S(2)}) copy-start(bf16[256,1536]{1,0:T(8,128)(2,1)} %param.7) | copy-start | bytes 2359300
Sparse Core Ops, SparseCore 0:
  257.9 31.9 reduce-scatter.1
